TPU v7x, 128 devices: a whole 4x4x4 slice. The times are simulated.
128 devices in a mesh: silo: 8 (over z, core), row: 16 (over y, x).
Axes of the slice: x: 4, y: 4, z: 4, core: 2. Of those that a mesh axis runs over, the one named last changes fastest.
Arguments:
- silo_grams: float32 [16, 4096, 4096], P('silo', 'row'), may hold values from -9 to 81, as said below
- silo_weights: bfloat16 [16, 4096, 640], P('silo', 'row'), may hold values from -6 to 6
Outputs:
- merged_rows: float32 [640, 4096], P(('silo', 'row'))
Inputs may be any that keep to these rules, and one draw needn't show every extreme that they name: `silo_grams`: each silo's Gram is symmetric up to float32 rounding and positive definite.
All inputs are finite; a program needn't handle non-finite values.
Results may differ from a plain program's by a relative error of at most 0.0003.
Values may be sent and summed in bfloat16 or wider, within the bound.
A program may use at most 128 MiB of HBM per device.

v0:
```python
import jax
import jax.numpy as jnp
from jax import lax
from jax.sharding import Mesh
from jax.sharding import PartitionSpec as P

ITERS = 2
ROW = ("row_0", "row_1")
SILO_ROW = ("silo", "row_0", "row_1")
full_precision = lax.Precision.HIGHEST


def in_blocks(value, dim, peers):
    lengths = value.shape
    parts = value.reshape(*lengths[:dim], peers, lengths[dim] // peers, *lengths[dim + 1 :])
    return jnp.moveaxis(parts, dim, 0)


def summed_on_arrival(value, axis, dim):
    parts = in_blocks(value, dim, lax.axis_size(axis))
    arrived = lax.all_to_all(parts, axis, split_axis=0, concat_axis=0, tiled=True)
    return arrived.sum(axis=0)


def joined_along(parts, dim):
    lengths = list(parts.shape[1:])
    lengths[dim] *= parts.shape[0]
    return jnp.moveaxis(parts, 0, dim).reshape(lengths)


def sent_to_all(value, axis):
    copies = jnp.broadcast_to(value, (lax.axis_size(axis), *value.shape))
    return lax.all_to_all(copies, axis, split_axis=0, concat_axis=0, tiled=True)


def gathered_copies(value, axis, dim):
    return joined_along(sent_to_all(value, axis), dim)


def one_axis_at_a_time(value, axes):
    for axis in axes:
        value = lax.psum(value, axis)
    return value


def conj_grad(right_side, apply_op, sum_squares, sum_curv):
    solution = jnp.zeros_like(right_side)
    residual = right_side
    direction = right_side
    res_norm = sum_squares(jnp.sum(residual * residual, axis=0))
    for iteration in range(ITERS):
        mapped = apply_op(direction)
        step_size = res_norm / sum_curv(jnp.sum(direction * mapped, axis=0))
        solution = solution + step_size * direction
        residual = residual - step_size * mapped
        if iteration + 1 < ITERS:
            next_norm = sum_squares(jnp.sum(residual * residual, axis=0))
            direction = residual + next_norm / res_norm * direction
            res_norm = next_norm
    return solution


def local(silo_grams, silo_weights):
    partial_op = jnp.sum(silo_grams, axis=0)
    partial_rhs = jnp.einsum(
        "srk,skc->rc",
        silo_grams,
        lax.all_gather(silo_weights, ROW, axis=1, tiled=True).astype(jnp.float32),
        precision=full_precision,
    )
    operator = lax.psum(partial_op, "silo")
    right_side = summed_on_arrival(partial_rhs, "silo", 1)

    def apply_cols(direction):
        return jnp.dot(operator, gathered_copies(direction, ROW, 0), precision=full_precision)

    def squares_cols(values):
        return one_axis_at_a_time(values, ROW)

    def curv_values(values):
        return one_axis_at_a_time(values, ROW)

    solution = conj_grad(right_side, apply_cols, squares_cols, curv_values)
    transposed = solution.T
    return lax.all_to_all(transposed, ROW, split_axis=0, concat_axis=1, tiled=True)


def solution(mesh):
    torus = Mesh(mesh.devices.reshape(mesh.shape["silo"], 4, 4), ("silo", "row_0", "row_1"))
    in_specs = (P("silo", ROW, None), P("silo", ROW, None))
    out_specs = P(SILO_ROW, None)
    return jax.shard_map(local, mesh=torus, in_specs=in_specs, out_specs=out_specs, check_vma=False)
```

profile of v0, /device:TPU:0, one launch (start us, length us, event | category | flops | bytes accessed | tf_op | source)
XLA Modules:
  0.0 250.4 jit_solution(15347304648735894825)
XLA Ops:
  7.4 0.7 all-gather.2.cloned.1.call-update
  8.1 6.4 %reduce_sum.56 = f32[256,4096]{1,0:T(8,128)} reduce(f32[2,256,4096]{2,1,0:T(8,128)} %param.2, f32[]{:T(128)} %constant.0.clone.1), dimensions={0}, to_apply=%region_4.0 | reduce | flops 1048576 | bytes 12582916 | tf_op jit(solution)/shard_map/reduce_sum | solution.py:64
  14.6 78.5 %all-gather.2.cloned.1.call-done = bf16[2,4096,640]{2,1,0:T(8,128)(2,1)} async-done(((bf16[2,256,640]{2,1,0:T(8,128)(2,1)}), bf16[2,4096,640]{2,1,0:T(8,128)(2,1)}) %all-gather.2.cloned.1.call-update) | async-done | bytes 10485776 | tf_op jit(solution)/shard_map/all_gather | solution.py:68
  93.1 15.7 %fusion.1 = f32[256,640,1]{0,1,2:T(8,128)S(1)} fusion(f32[2,256,4096]{2,1,0:T(8,128)} %param.2, bf16[2,4096,640]{2,1,0:T(8,128)(2,1)} %all-gather.2.cloned.1.call-done), kind=kOutput, calls=%fused_computation.8 | convolution fusion | flops 16106127360 | bytes 19529728 | tf_op jit(solution)/shard_map/srk,skc->rc/dot_general | solution.py:65
  108.8 16.0 %all_to_all.34 = f32[8,256,80]{1,2,0:T(8,128)S(1)} all-to-all(f32[8,256,80]{1,2,0:T(8,128)S(1)} %bitcast.24), channel_id=1, replica_groups=mesh['silo'=8,'row_0'=4,'row_1'=4] {'silo'}, dimensions={0} | all-to-all | bytes 1310720 | tf_op jit(solution)/shard_map/all_to_all | solution.py:21
  124.9 0.1 broadcast_in_dim.4
  125.0 24.9 %all_to_all.35 = f32[16,256,80]{1,2,0:T(8,128)S(1)} all-to-all(f32[16,256,80]{1,2,0:T(8,128)S(1)} %broadcast_in_dim.4), channel_id=1, replica_groups=mesh['silo'=8,'row_0'=4,'row_1'=4] {'row_0','row_1'}, dimensions={0} | all-to-all | bytes 2621440 | tf_op jit(solution)/shard_map/all_to_all | solution.py:33
  149.9 0.1 copy.14
  150.0 6.2 %multiply_reduce_fusion.1 = (f32[80]{0:T(128)S(1)}, f32[80]{0:T(128)S(1)}, f32[256,80]{0,1:T(8,128)S(1)}) fusion(f32[256,80]{0,1:T(8,128)S(1)} %reduce_sum.54, f32[256,4096]{1,0:T(8,128)} %all-reduce.4.cloned.1.call-done, f32[4096,80]{0,1:T(8,128)S(1)} %bitcast.22), kind=kOutput, calls=%fused_computation.6 | convolution fusion | flops 1006714752 | bytes 5669504 | tf_op jit(solution)/shard_map/dot_general | solution.py:75
  156.3 8.6 %all-reduce.1 = (f32[80]{0:T(128)S(1)}, f32[80]{0:T(128)S(1)}) all-reduce(f32[80]{0:T(128)S(1)} %get-tuple-element.6, f32[80]{0:T(128)S(1)} %get-tuple-element.5), channel_id=1, replica_groups=mesh['silo'=8,'row_0'=4,'row_1'=4] {'row_0'}, use_global_device_ids=true, to_apply=%region_2.0 | all-reduce | flops 160 | bytes 1280 | tf_op jit(solution)/shard_map/psum | solution.py:42
  164.9 8.7 %all-reduce = (f32[80]{0:T(128)S(1)}, f32[80]{0:T(128)S(1)}) all-reduce(f32[80]{0:T(128)S(1)} %get-tuple-element.9, f32[80]{0:T(128)S(1)} %get-tuple-element.10), channel_id=1, replica_groups=mesh['silo'=8,'row_0'=4,'row_1'=4] {'row_1'}, use_global_device_ids=true, to_apply=%region_3.0 | all-reduce | flops 160 | bytes 1280 | tf_op jit(solution)/shard_map/psum | solution.py:42
  173.6 0.2 multiply_reduce_fusion
  173.8 8.6 %psum.68 = f32[80]{0:T(128)S(1)} all-reduce(f32[80]{0:T(128)S(1)} %multiply_reduce_fusion), channel_id=1, replica_groups=mesh['silo'=8,'row_0'=4,'row_1'=4] {'row_0'}, use_global_device_ids=true, to_apply=%region_10.0 | all-reduce | flops 80 | bytes 640 | tf_op jit(solution)/shard_map/psum | solution.py:42
  182.4 9.1 %psum.69 = f32[80]{0:T(128)S(1)} all-reduce(f32[80]{0:T(128)S(1)} %psum.68), channel_id=1, replica_groups=mesh['silo'=8,'row_0'=4,'row_1'=4] {'row_1'}, use_global_device_ids=true, to_apply=%region_11.0 | all-reduce | flops 80 | bytes 640 | tf_op jit(solution)/shard_map/psum | solution.py:42
  191.5 0.1 multiply_add_fusion
  191.6 0.1 broadcast_in_dim.5
  191.8 18.1 %all_to_all.36 = f32[16,256,80]{1,2,0:T(8,128)S(1)} all-to-all(f32[16,256,80]{1,2,0:T(8,128)S(1)} %broadcast_in_dim.5), channel_id=1, replica_groups=mesh['silo'=8,'row_0'=4,'row_1'=4] {'row_0','row_1'}, dimensions={0} | all-to-all | bytes 2621440 | tf_op jit(solution)/shard_map/all_to_all | solution.py:33
  209.9 0.1 copy.15
  210.0 4.0 %fusion = f32[80]{0:T(128)S(1)} fusion(f32[256,80]{0,1:T(8,128)S(1)} %multiply_add_fusion, f32[256,4096]{1,0:T(8,128)S(1)} %copy-done, f32[4096,80]{0,1:T(8,128)S(1)} %bitcast.23), kind=kOutput, calls=%fused_computation.1 | convolution fusion | flops 1006673856 | bytes 5587264 | tf_op jit(solution)/shard_map/dot_general | solution.py:75
  214.0 8.6 %psum.70 = f32[80]{0:T(128)S(1)} all-reduce(f32[80]{0:T(128)S(1)} %fusion), channel_id=1, replica_groups=mesh['silo'=8,'row_0'=4,'row_1'=4] {'row_0'}, use_global_device_ids=true, to_apply=%region_13.0 | all-reduce | flops 80 | bytes 640 | tf_op jit(solution)/shard_map/psum | solution.py:42
  222.6 8.7 %psum.71 = f32[80]{0:T(128)S(1)} all-reduce(f32[80]{0:T(128)S(1)} %psum.70), channel_id=1, replica_groups=mesh['silo'=8,'row_0'=4,'row_1'=4] {'row_1'}, use_global_device_ids=true, to_apply=%region_14.0 | all-reduce | flops 80 | bytes 640 | tf_op jit(solution)/shard_map/psum | solution.py:42
  231.3 0.1 add_bitcast_fusion
  231.5 10.8 %all_to_all.37 = f32[16,5,256]{2,1,0:T(8,128)S(1)} all-to-all(f32[16,5,256]{2,1,0:T(8,128)S(1)} %all_to_all.26), channel_id=1, replica_groups=mesh['silo'=8,'row_0'=4,'row_1'=4] {'row_0','row_1'}, dimensions={0} | all-to-all | bytes 163840 | tf_op jit(solution)/shard_map/all_to_all | solution.py:85
  242.3 0.7 copy.18
  (11 shorter events, 0.2 us)
Async XLA Ops:
  7.4 85.7 %all-gather.2.cloned.1.call-start = ((), (), s32[]{:S(2)}) async-start(), calls=%async_computation.4 | async-start | bytes 11141120 | tf_op jit(solution)/shard_map/all_gather | solution.py:68
  8.1 141.9 %all-reduce.4.cloned.1.call-start = ((), (), s32[]{:S(2)}) async-start(), calls=%async_computation.5 | async-start | bytes 8388608 | tf_op jit(solution)/shard_map/psum | solution.py:71
  191.5 18.5 %copy-start = (f32[256,4096]{1,0:T(8,128)S(1)}, f32[256,4096]{1,0:T(8,128)}, u32[]{:S(2)}) copy-start(f32[256,4096]{1,0:T(8,128)} %all-reduce.4.cloned.1.call-done) | copy-start | bytes 12582916
Sparse Core Ops, SparseCore 0:
  10.3 82.7 all-gather.1
Sparse Core Ops, SparseCore 1:
  14.7 76.3 all-reduce.3
where the time goes:
time: 251 us; the launch traced here: 250 us
  blocking collectives  122 us (49%)
  waiting for transfers between devices  79.3 us (32%)
  matrix products  26 us (10%)
  between operations  14.9 us (6%)
  other arithmetic  6.85 us (3%)
    all_gather x1, waiting for transfers between devices, local(): lax.all_gather(silo_weights, ROW, axis=1, tiled=True).astype(jnp.float32)  78.5 us
    psum x6, blocking collectives, one_axis_at_a_time(): value = lax.psum(value, axis)  52.3 us
    all_to_all x2, blocking collectives, sent_to_all(): return lax.all_to_all(copies, axis, split_axis=0, concat_axis=0, tiled=True)  43 us
    all_to_all x1, blocking collectives, summed_on_arrival(): lax.all_to_all(parts, axis, split_axis=0, concat_axis=0, tiled=True)  16 us
    dot_general x1, matrix products, local(): jnp.einsum('srk,skc->rc', silo_grams, lax.all_gather(silo_weights, ROW, a...  15.7 us
    all_to_all x1, blocking collectives, local(): lax.all_to_all(transposed, ROW, split_axis=0, concat_axis=1, tiled=True)  10.8 us
    dot_general x2, matrix products, apply_cols(): jnp.dot(operator, gathered_copies(direction, ROW, 0), precision=full_prec...  10.3 us
    reduce_sum x1, other arithmetic, local(): partial_op = jnp.sum(silo_grams, axis=0)  6.42 us
  transfers between devices with their start and end apart: 2, of which 1 were waited for; matrix products, arithmetic and copies ran while one was open for 9% of the time, Pallas kernels for 0%

commit v1 on v0

--- a/solution.py
+++ b/solution.py
@@ -65,7 +65,9 @@
     partial_rhs = jnp.einsum(
         "srk,skc->rc",
         silo_grams,
-        lax.all_gather(silo_weights, ROW, axis=1, tiled=True).astype(jnp.float32),
+        jnp.concatenate(
+            lax.all_to_all(jnp.stack([silo_weights] * lax.axis_size(ROW)), ROW, 0, 0), axis=1
+        ).astype(jnp.float32),
         precision=full_precision,
     )
     operator = lax.psum(partial_op, "silo")

time: 251 us -> 355 us (1.41)
  waiting for transfers between devices: 79.3 us -> 149 us
  local copies, waits for them, and re-layouts: 1.16 us -> 31.6 us
  starting transfers between devices: 0.05 us -> 7.2 us
    all_to_all x0 -> x1, waiting for transfers between devices: none -> 149 us  [local(): lax.all_to_all(jnp.stack([silo_weights] * lax.axis_size(ROW)), ROW, 0, 0)]
    all_gather x1 -> x0, waiting for transfers between devices: 78.5 us -> none  [local(): lax.all_gather(silo_weights, ROW, axis=1, tiled=True).astype(jnp.float32)]
    dot_general x0 -> x1, local copies, waits for them, and re-layouts: none -> 14.7 us  [local(): jnp.einsum('srk,skc->rc', silo_grams, jnp.concatenate(lax.all_to_all(jnp....]
    all_to_all x0 -> x1, local copies, waits for them, and re-layouts: none -> 9.4 us  [local(): lax.all_to_all(jnp.stack([silo_weights] * lax.axis_size(ROW)), ROW, 0, 0)]
    all_to_all x0 -> x1, starting transfers between devices: none -> 7.16 us  [local(): lax.all_to_all(jnp.stack([silo_weights] * lax.axis_size(ROW)), ROW, 0, 0)]
    another operation x0 -> x1, local copies, waits for them, and re-layouts: none -> 6.34 us  [local(): jnp.stack([silo_weights] * lax.axis_size(ROW))]
  transfers between devices with their start and end apart: 2 -> 2, of which waited for: 1 -> 1; matrix products, arithmetic and copies ran while one was open for 9% -> 12% of each run, Pallas kernels for 0% -> 0%
where the time goes in v1:
time: 355 us; the launch traced here: 354 us
  waiting for transfers between devices  149 us (42%)
  blocking collectives  123 us (35%)
  local copies, waits for them, and re-layouts  31.6 us (9%)
  matrix products  22.7 us (6%)
  between operations  13.5 us (4%)
  starting transfers between devices  7.2 us (2%)
  other arithmetic  6.85 us (2%)
    all_to_all x1, waiting for transfers between devices, local(): lax.all_to_all(jnp.stack([silo_weights] * lax.axis_size(ROW)), ROW, 0, 0)  149 us
    psum x6, blocking collectives, one_axis_at_a_time(): value = lax.psum(value, axis)  52.4 us
    all_to_all x2, blocking collectives, sent_to_all(): return lax.all_to_all(copies, axis, split_axis=0, concat_axis=0, tiled=True)  42.9 us
    all_to_all x1, blocking collectives, summed_on_arrival(): lax.all_to_all(parts, axis, split_axis=0, concat_axis=0, tiled=True)  16.9 us
    dot_general x1, local copies, waits for them, and re-layouts, local(): jnp.einsum('srk,skc->rc', silo_grams, jnp.concatenate(lax.all_to_all(jnp....  14.7 us
    dot_general x1, matrix products, local(): jnp.einsum('srk,skc->rc', silo_grams, jnp.concatenate(lax.all_to_all(jnp....  12.4 us
    all_to_all x1, blocking collectives, local(): lax.all_to_all(transposed, ROW, split_axis=0, concat_axis=1, tiled=True)  10.8 us
    dot_general x2, matrix products, apply_cols(): jnp.dot(operator, gathered_copies(direction, ROW, 0), precision=full_prec...  10.3 us
  transfers between devices with their start and end apart: 2, of which 1 were waited for; matrix products, arithmetic and copies ran while one was open for 12% of the time, Pallas kernels for 0%

profile of v1, /device:TPU:0, one launch (start us, length us, event | category | flops | bytes accessed | tf_op | source)
XLA Modules:
  0.0 353.7 jit_solution(7727881292983721413)
XLA Ops:
  6.5 6.3 %stack.2 = bf16[16,2,256,640]{3,2,1,0:T(8,128)(2,1)} broadcast(bf16[2,256,640]{2,1,0:T(8,128)(2,1)} %param.3), dimensions={1,2,3} | broadcast | bytes 11141120 | tf_op jit(solution)/shard_map/stack | solution.py:69
  12.9 7.2 %all-to-all-start = ((bf16[16,2,256,640]{3,2,1,0:T(8,128)(2,1)}), bf16[16,2,256,640]{3,2,1,0:T(8,128)(2,1)}, u32[]{:S(2)}, u32[]{:S(2)}) async-start(bf16[16,2,256,640]{3,2,1,0:T(8,128)(2,1)} %stack.2), calls=%async_computation | async-start | bytes 20971520 | tf_op jit(solution)/shard_map/all_to_all | solution.py:69
  20.1 6.4 %reduce_sum.56 = f32[256,4096]{1,0:T(8,128)} reduce(f32[2,256,4096]{2,1,0:T(8,128)} %param.2, f32[]{:T(128)} %constant.0.clone.1), dimensions={0}, to_apply=%region_4.0 | reduce | flops 1048576 | bytes 12582916 | tf_op jit(solution)/shard_map/reduce_sum | solution.py:64
  26.5 148.9 %all-to-all-done = bf16[16,2,256,640]{3,2,1,0:T(8,128)(2,1)} async-done(((bf16[16,2,256,640]{3,2,1,0:T(8,128)(2,1)}), bf16[16,2,256,640]{3,2,1,0:T(8,128)(2,1)}, u32[]{:S(2)}, u32[]{:S(2)}) %all-to-all-start) | async-done | bytes 10485792 | tf_op jit(solution)/shard_map/all_to_all | solution.py:69
  175.5 9.4 %copy.12 = bf16[16,2,256,640]{3,2,0,1:T(8,128)(2,1)} copy(bf16[16,2,256,640]{3,2,1,0:T(8,128)(2,1)} %all-to-all-done) | data formatting | bytes 20971520 | tf_op jit(solution)/shard_map/all_to_all | solution.py:69
  184.8 14.7 %copy.13 = bf16[640,4096,2]{1,0,2:T(8,128)(2,1)} copy(bf16[640,4096,2]{0,1,2:T(8,128)(2,1)} %bitcast.35) | data formatting | bytes 20971520 | tf_op jit(solution)/shard_map/srk,skc->rc/dot_general | solution.py:65
  199.6 12.4 %fusion.2 = f32[8,256,80]{1,2,0:T(8,128)S(1)} fusion(bf16[8,80,4096,2]{2,1,0,3:T(8,128)(2,1)} %bitcast.36, f32[2,256,4096]{2,1,0:T(8,128)} %param.2), kind=kOutput, calls=%fused_computation.2 | convolution fusion | flops 16106127360 | bytes 19529728 | tf_op jit(solution)/shard_map/srk,skc->rc/dot_general | solution.py:65
  212.0 16.9 %all_to_all.39 = f32[8,256,80]{1,2,0:T(8,128)S(1)} all-to-all(f32[8,256,80]{1,2,0:T(8,128)S(1)} %fusion.2), channel_id=1, replica_groups=mesh['silo'=8,'row_0'=4,'row_1'=4] {'silo'}, dimensions={0} | all-to-all | bytes 1310720 | tf_op jit(solution)/shard_map/all_to_all | solution.py:21
  229.0 0.1 broadcast_in_dim.4
  229.1 24.8 %all_to_all.40 = f32[16,256,80]{1,2,0:T(8,128)S(1)} all-to-all(f32[16,256,80]{1,2,0:T(8,128)S(1)} %broadcast_in_dim.4), channel_id=1, replica_groups=mesh['silo'=8,'row_0'=4,'row_1'=4] {'row_0','row_1'}, dimensions={0} | all-to-all | bytes 2621440 | tf_op jit(solution)/shard_map/all_to_all | solution.py:33
  253.9 0.1 copy.18
  254.0 6.2 %multiply_reduce_fusion.1 = (f32[80]{0:T(128)S(1)}, f32[80]{0:T(128)S(1)}, f32[256,80]{0,1:T(8,128)S(1)}) fusion(f32[256,80]{0,1:T(8,128)S(1)} %reduce_sum.54, f32[256,4096]{1,0:T(8,128)} %all-reduce.4.cloned.1.call-done, f32[4096,80]{0,1:T(8,128)S(1)} %bitcast.39), kind=kOutput, calls=%fused_computation.9 | convolution fusion | flops 1006714752 | bytes 5669504 | tf_op jit(solution)/shard_map/dot_general | solution.py:77
  260.3 8.6 %all-reduce.1 = (f32[80]{0:T(128)S(1)}, f32[80]{0:T(128)S(1)}) all-reduce(f32[80]{0:T(128)S(1)} %get-tuple-element.6, f32[80]{0:T(128)S(1)} %get-tuple-element.5), channel_id=1, replica_groups=mesh['silo'=8,'row_0'=4,'row_1'=4] {'row_0'}, use_global_device_ids=true, to_apply=%region_2.0 | all-reduce | flops 160 | bytes 1280 | tf_op jit(solution)/shard_map/psum | solution.py:42
  268.9 8.7 %all-reduce = (f32[80]{0:T(128)S(1)}, f32[80]{0:T(128)S(1)}) all-reduce(f32[80]{0:T(128)S(1)} %get-tuple-element.9, f32[80]{0:T(128)S(1)} %get-tuple-element.10), channel_id=1, replica_groups=mesh['silo'=8,'row_0'=4,'row_1'=4] {'row_1'}, use_global_device_ids=true, to_apply=%region_3.0 | all-reduce | flops 160 | bytes 1280 | tf_op jit(solution)/shard_map/psum | solution.py:42
  277.6 0.2 multiply_reduce_fusion
  277.8 8.6 %psum.68 = f32[80]{0:T(128)S(1)} all-reduce(f32[80]{0:T(128)S(1)} %multiply_reduce_fusion), channel_id=1, replica_groups=mesh['silo'=8,'row_0'=4,'row_1'=4] {'row_0'}, use_global_device_ids=true, to_apply=%region_10.0 | all-reduce | flops 80 | bytes 640 | tf_op jit(solution)/shard_map/psum | solution.py:42
  286.4 9.1 %psum.69 = f32[80]{0:T(128)S(1)} all-reduce(f32[80]{0:T(128)S(1)} %psum.68), channel_id=1, replica_groups=mesh['silo'=8,'row_0'=4,'row_1'=4] {'row_1'}, use_global_device_ids=true, to_apply=%region_11.0 | all-reduce | flops 80 | bytes 640 | tf_op jit(solution)/shard_map/psum | solution.py:42
  295.8 18.1 %all_to_all.41 = f32[16,256,80]{1,2,0:T(8,128)S(1)} all-to-all(f32[16,256,80]{1,2,0:T(8,128)S(1)} %broadcast_in_dim.5), channel_id=1, replica_groups=mesh['silo'=8,'row_0'=4,'row_1'=4] {'row_0','row_1'}, dimensions={0} | all-to-all | bytes 2621440 | tf_op jit(solution)/shard_map/all_to_all | solution.py:33
  313.8 0.1 copy.19
  314.0 4.0 %fusion.5 = f32[80]{0:T(128)S(1)} fusion(f32[256,80]{0,1:T(8,128)S(1)} %multiply_add_fusion, f32[256,4096]{1,0:T(8,128)S(1)} %copy-done, f32[4096,80]{0,1:T(8,128)S(1)} %bitcast.40), kind=kOutput, calls=%fused_computation.4 | convolution fusion | flops 1006673856 | bytes 5587264 | tf_op jit(solution)/shard_map/dot_general | solution.py:77
  318.0 8.6 %psum.70 = f32[80]{0:T(128)S(1)} all-reduce(f32[80]{0:T(128)S(1)} %fusion.5), channel_id=1, replica_groups=mesh['silo'=8,'row_0'=4,'row_1'=4] {'row_0'}, use_global_device_ids=true, to_apply=%region_13.0 | all-reduce | flops 80 | bytes 640 | tf_op jit(solution)/shard_map/psum | solution.py:42
  326.6 8.7 %psum.71 = f32[80]{0:T(128)S(1)} all-reduce(f32[80]{0:T(128)S(1)} %psum.70), channel_id=1, replica_groups=mesh['silo'=8,'row_0'=4,'row_1'=4] {'row_1'}, use_global_device_ids=true, to_apply=%region_14.0 | all-reduce | flops 80 | bytes 640 | tf_op jit(solution)/shard_map/psum | solution.py:42
  335.4 10.8 %all_to_all.42 = f32[16,5,256]{2,1,0:T(8,128)S(1)} all-to-all(f32[16,5,256]{2,1,0:T(8,128)S(1)} %all_to_all.30), channel_id=1, replica_groups=mesh['silo'=8,'row_0'=4,'row_1'=4] {'row_0','row_1'}, dimensions={0} | all-to-all | bytes 163840 | tf_op jit(solution)/shard_map/all_to_all | solution.py:87
  346.2 0.7 copy.22
  (13 shorter events, 0.5 us)
Async XLA Ops:
  12.9 162.6 %all-to-all-start = ((bf16[16,2,256,640]{3,2,1,0:T(8,128)(2,1)}), bf16[16,2,256,640]{3,2,1,0:T(8,128)(2,1)}, u32[]{:S(2)}, u32[]{:S(2)}) async-start(bf16[16,2,256,640]{3,2,1,0:T(8,128)(2,1)} %stack.2), calls=%async_computation | async-start | bytes 20971520 | tf_op jit(solution)/shard_map/all_to_all | solution.py:69
  20.0 234.0 %all-reduce.4.cloned.1.call-start = ((), (), s32[]{:S(2)}) async-start(), calls=%async_computation.5 | async-start | bytes 8388608 | tf_op jit(solution)/shard_map/psum | solution.py:73
  295.5 18.5 %copy-start = (f32[256,4096]{1,0:T(8,128)S(1)}, f32[256,4096]{1,0:T(8,128)}, u32[]{:S(2)}) copy-start(f32[256,4096]{1,0:T(8,128)} %all-reduce.4.cloned.1.call-done) | copy-start | bytes 12582916
Sparse Core Ops, SparseCore 0:
  26.7 77.1 all-reduce.3
